TPU v7x, 32 devices: a whole 2x2x4 slice. The times are simulated.
32 devices in a mesh: clip: 2 (over y), tm: 8 (over z, x), tile: 2 (over core).
Axes of the slice: x: 2, y: 2, z: 4, core: 2. Of those that a mesh axis runs over, the one named last changes fastest.
Arguments:
- queries: bfloat16 [32, 256, 2048], P(('clip', 'tm'), 'tile'), parts along dimension 0, may hold values from -48 to 48
- keyvals: bfloat16 [2, 32, 256, 512], P(None, ('clip', 'tm'), 'tile'), parts along dimension 1, may hold values from -4 to 4
- proj_weight: bfloat16 [2048, 1024], P('tm', 'tile'), may hold values from -0.125 to 0.125
- norm_gain: float32 [1024], P('tile'), may hold values from 0.25 to 1.75
- frame_counts: int32 [32], P(('clip', 'tm')), parts along dimension 0, may hold values from 129 to 256, as said below
Outputs:
- dynamics: bfloat16 [32, 256, 1024], P(('clip', 'tm'), None, 'tile'), parts along dimension 0
There are 2 independent parts, one for each index of `clip`. A program takes and returns all parts, laid end to end along the dimension named above; an argument that names none is the same for every part. Nothing has to cross between parts.
Inputs may be any that keep to these rules, and one draw needn't show every extreme that they name: `frame_counts`: every spatial tile of every frame holds a live slot; some frame is full.
All inputs are finite; a program needn't handle non-finite values.
Results may differ from a plain program's by a relative error of at most 0.013.
Values may be sent and summed in bfloat16 or wider, within the bound.
A program may use at most 64 MiB of HBM per device.

v0:
```python
import jax
import jax.numpy as jnp
from jax import lax
from jax.sharding import PartitionSpec as P

QHEADS = 16
KVHEADS = 4
HEAD_DIM = 128
IDM_DIM = 64
WINDOW = 4
PARTNER = 16


def passed_along(value, axis, steps):
    count = lax.axis_size(axis)
    initial, last = (max(0, -steps), min(count, count - steps))
    return lax.ppermute(value, axis, [(source, source + steps) for source in range(initial, last)])


def window_attention(query_block, key_block, value_block, live_keys, groups):
    row_count = query_block.shape[0]
    key_heads = key_block.shape[1]
    head_width = key_block.shape[2]
    grouped = query_block.reshape(row_count, key_heads, groups, head_width)
    scores = jnp.einsum(
        "ikgd,jkd->ikgj", grouped, key_block, preferred_element_type=jnp.float32
    ) * head_width ** (-0.5)
    key_mask = live_keys[None, None, None, :]
    row_max = jnp.max(jnp.where(key_mask, scores, -1e30), axis=-1, keepdims=True)
    weights = jnp.where(key_mask, jnp.exp(jnp.where(key_mask, scores, row_max) - row_max), 0.0)
    normalized = (weights / jnp.sum(weights, axis=-1, keepdims=True)).astype(jnp.bfloat16)
    blended = jnp.einsum(
        "ikgj,jkd->ikgd", normalized, value_block, preferred_element_type=jnp.float32
    )
    return blended.astype(jnp.bfloat16).reshape(row_count, key_heads * groups * head_width)


def normalize_heads(latent_block, gain):
    width = latent_block.shape[-1]
    heads = width // IDM_DIM
    values = latent_block.astype(jnp.float32).reshape(latent_block.shape[:-1] + (heads, IDM_DIM))
    scaled = values * lax.rsqrt(jnp.mean(values * values, axis=-1, keepdims=True) + 1e-06)
    scaled = scaled * gain.reshape(heads, IDM_DIM)
    return scaled.astype(jnp.bfloat16).reshape(latent_block.shape)


def local(queries, keyvals, proj_weight, norm_gain, frame_counts):
    frames_here = queries.shape[0]
    tile_tokens = queries.shape[1]
    groups = QHEADS // KVHEADS
    lead_frames = WINDOW - 1
    hop_total = (lead_frames + frames_here - 1) // frames_here
    tile_place = lax.axis_index("tile")
    received = []
    for hop_count in range(1, hop_total + 1):
        needed = min(frames_here, lead_frames - (hop_count - 1) * frames_here)
        piece_pair = passed_along(
            (keyvals[:, frames_here - needed :], frame_counts[frames_here - needed :]),
            "tm",
            hop_count,
        )
        received = [piece_pair] + received
    earlier_kv = jnp.concatenate([received_pair[0] for received_pair in received], axis=1)
    earlier_counts = jnp.concatenate([received_pair[1] for received_pair in received], axis=0)
    window_kv = jnp.concatenate([earlier_kv, keyvals], axis=1)
    window_counts = jnp.concatenate([earlier_counts, frame_counts], axis=0)
    slot_index = tile_place * tile_tokens + jnp.arange(tile_tokens, dtype=jnp.int32)
    attended_frames = []
    for frame_index in range(frames_here):
        block_kv = window_kv[:, frame_index : frame_index + WINDOW]
        live_keys = (
            slot_index[None, :] < window_counts[frame_index : frame_index + WINDOW, None]
        ).reshape(WINDOW * tile_tokens)
        key_block = block_kv[0].reshape(WINDOW * tile_tokens, KVHEADS, HEAD_DIM)
        value_block = block_kv[1].reshape(WINDOW * tile_tokens, KVHEADS, HEAD_DIM)
        attended_frames.append(
            window_attention(queries[frame_index], key_block, value_block, live_keys, groups)
        )
    attended = jnp.stack(attended_frames)
    query_width = attended.shape[2]
    full_columns = lax.all_gather(proj_weight, "tile", axis=1, tiled=True)
    token_rows = attended.reshape(frames_here * tile_tokens, query_width)
    summed = jnp.dot(
        token_rows,
        lax.all_gather(full_columns, "tm", axis=0, tiled=True),
        preferred_element_type=jnp.float32,
    )
    own_latent = summed.astype(jnp.bfloat16).reshape(
        frames_here, tile_tokens, full_columns.shape[1]
    )
    latent = lax.all_to_all(own_latent, "tile", split_axis=2, concat_axis=1, tiled=True)
    normed = normalize_heads(latent, norm_gain)
    frame_tokens = normed.shape[1]
    heads_here = normed.shape[2] // IDM_DIM
    distance = PARTNER // frames_here
    before_normed, before_counts = passed_along((normed, frame_counts), "tm", distance)
    after_normed, after_counts = passed_along((normed, frame_counts), "tm", -distance)
    slot_all = jnp.arange(frame_tokens, dtype=jnp.int32)
    results = []
    for frame_index in range(frames_here):
        key_rows = jnp.concatenate(
            [before_normed[frame_index], normed[frame_index], after_normed[frame_index]], axis=0
        )
        key_rows = key_rows.reshape(3 * frame_tokens, heads_here, IDM_DIM)
        live_keys = jnp.concatenate(
            [
                slot_all < before_counts[frame_index],
                slot_all < frame_counts[frame_index],
                slot_all < after_counts[frame_index],
            ]
        )
        query_rows = normed[frame_index].reshape(frame_tokens, heads_here, IDM_DIM)
        scores = jnp.einsum(
            "ihd,jhd->ihj", query_rows, key_rows, preferred_element_type=jnp.float32
        ) * IDM_DIM ** (-0.5)
        weights = jnp.where(live_keys[None, None, :], jnp.exp(scores), 0.0)
        normalized = (weights / jnp.sum(weights, axis=-1, keepdims=True)).astype(jnp.bfloat16)
        blended = jnp.einsum(
            "ihj,jhd->ihd", normalized, key_rows, preferred_element_type=jnp.float32
        )
        results.append(blended.astype(jnp.bfloat16).reshape(frame_tokens, heads_here * IDM_DIM))
    return jnp.stack(results)


def solution(mesh):
    in_specs = (
        P(("clip", "tm"), "tile", None),
        P(None, ("clip", "tm"), "tile", None),
        P("tm", "tile"),
        P("tile"),
        P(("clip", "tm")),
    )
    out_specs = P(("clip", "tm"), None, "tile")
    return jax.shard_map(local, mesh=mesh, in_specs=in_specs, out_specs=out_specs, check_vma=False)
```

profile of v0, /device:TPU:0, one launch (start us, length us, event | category | flops | bytes accessed | tf_op | source)
XLA Modules:
  0.0 125.4 jit_solution(14114580612585396030)
XLA Ops:
  6.5 0.0 all-gather.2.cloned.1.call-start
  6.5 4.3 %all_gather.6 = bf16[256,1024]{1,0:T(8,128)(2,1)} all-gather(bf16[256,512]{1,0:T(8,128)(2,1)} %param.7), channel_id=1, replica_groups=mesh['clip'=2,'tm'=8,'tile'=2] {'tile'}, dimensions={1}, use_global_device_ids=true | all-gather | bytes 786432 | tf_op jit(solution)/shard_map/all_gather | solution.py:81
  10.8 0.0 all-gather.2.cloned.1.call-update
  10.9 4.5 %collective-permute-start.3 = (s32[2]{0:T(128)}, s32[2]{0:T(128)S(1)}, u32[]{:S(2)}, u32[]{:S(2)}) collective-permute-start(s32[2]{0:T(128)} %param.9), channel_id=1, source_target_pairs={{0,2},{2,4},{4,6},{6,8},{8,10},{10,12},{12,14},{1,3},{3,5},{5,7},{... | collective-permute-start | bytes 32 | tf_op jit(solution)/shard_map/ppermute | solution.py:17
  15.4 0.7 collective-permute-start.5
  16.0 3.5 %collective-permute-start.1 = (bf16[2,2,128,512]{3,2,1,0:T(8,128)(2,1)}, bf16[2,2,128,512]{3,2,1,0:T(8,128)(2,1)S(1)}, u32[]{:S(2)}, u32[]{:S(2)}) collective-permute-start(bf16[2,2,128,512]{3,2,1,0:T(8,128)(2,1)} %param.6), channel_id=1, source_target_pairs={{0,2},{2,4},{4,6},{6,8},{8,10},{10,12},{12,14},{1,3},{3,5},{5,7},{... | collective-permute-start | bytes 1572872 | tf_op jit(solution)/shard_map/ppermute | solution.py:17
  19.5 1.0 slice.65
  20.5 3.5 %collective-permute-start = (bf16[2,1,128,512]{3,2,1,0:T(8,128)(2,1)S(1)}, bf16[2,1,128,512]{3,2,1,0:T(8,128)(2,1)S(1)}, u32[]{:S(2)}, u32[]{:S(2)}) collective-permute-start(bf16[2,1,128,512]{3,2,1,0:T(8,128)(2,1)S(1)} %slice.65), channel_id=1, source_target_pairs={{0,4},{2,6},{4,8},{6,10},{8,12},{10,14},{1,5},{3,7},{5,9},{7,11},{... | collective-permute-start | bytes 786440 | tf_op jit(solution)/shard_map/ppermute | solution.py:17
  24.0 1.4 %fusion.52 = (s32[1]{0:T(128)}, s32[1]{0:T(128)}) fusion(s32[2]{0:T(128)} %param.9), kind=kLoop, calls=%fused_computation.86 | loop fusion | bytes 16 | tf_op jit(solution)/shard_map/slice | solution.py:108
  25.4 4.0 %collective-permute-start.2 = (s32[1]{0:T(128)}, s32[1]{0:T(128)}, u32[]{:S(2)}, u32[]{:S(2)}) collective-permute-start(s32[1]{0:T(128)} %get-tuple-element.20), channel_id=1, source_target_pairs={{0,4},{2,6},{4,8},{6,10},{8,12},{10,14},{1,5},{3,7},{5,9},{7,11},{... | collective-permute-start | bytes 20 | tf_op jit(solution)/shard_map/ppermute | solution.py:17
  29.4 1.3 %fusion.49 = (bf16[1,128,2048]{2,1,0:T(8,128)(2,1)S(1)}, bf16[1,128,2048]{2,1,0:T(8,128)(2,1)S(1)}) fusion(bf16[2,128,2048]{2,1,0:T(8,128)(2,1)} %param.5), kind=kLoop, calls=%fused_computation.83 | loop fusion | bytes 2097152 | tf_op jit(solution)/shard_map/slice | solution.py:77
  30.7 0.3 copy.70
  31.0 0.3 copy.71
  31.3 0.0 copy-done.1
  31.3 0.1 mul.66
  31.4 0.6 iota_compare_fusion
  32.0 0.0 collective-permute-done.5
  32.0 0.7 fusion.53
  32.7 0.7 iota_compare_fusion.1
  33.4 1.3 %iota_compare_fusion.2 = (pred[256]{0:T(512)(128)(4,1)S(1)}, pred[256]{0:T(512)(128)(4,1)S(1)}) fusion(s32[]{:T(128)} %bitcast.22, s32[]{:T(128)} %bitcast.21), kind=kLoop, calls=%fused_computation.65 | loop fusion | flops 512 | bytes 520 | tf_op jit(solution)/shard_map/lt | solution.py:108
  34.7 0.0 collective-permute-done.3
  34.7 0.0 copy-done.2
  34.7 0.1 pad_add_fusion.3
  34.8 1.1 collective-permute-done.2
  35.9 0.8 pad_add_fusion.2
  36.6 0.1 compare_bitcast_fusion.1
  36.7 0.0 collective-permute-done
  36.7 0.1 collective-permute-done.1
  36.9 0.1 constant_dynamic-update-slice_fusion.1
  36.9 0.0 copy-done
  37.0 0.1 constant_dynamic-update-slice_fusion
  37.1 0.2 fusion.48
  37.2 0.9 reshape_squeeze.21
  38.2 0.1 reshape.102
  38.3 1.8 %fusion.6 = (f32[128,4,4]{0,2,1:T(4,128)S(1)}, f32[4,512,128,4]{2,1,3,0:T(8,128)S(1)}) fusion(pred[512]{0:T(512)(128)(4,1)S(1)} %get-tuple-element.23, bf16[128,4,4,128]{0,3,2,1:T(8,128)(2,1)S(1)} %bitcast.120, bf16[512,4,128,1]{2,1,0,3:T(4,128)(2,1)} %bitcast.122), kind=kOutput, calls=%fused_computation.16 | convolution fusion | flops 271579136 | bytes 5251584 | tf_op jit(solution)/shard_map/ikgd,jkd->ikgj/dot_general | solution.py:25
  40.1 1.1 fusion.14
  41.2 1.4 %fusion.19 = bf16[4,128,128,4]{2,1,3,0:T(8,128)(2,1)S(1)} fusion(f32[4,512,128,4]{2,1,3,0:T(8,128)S(1)} %get-tuple-element.28, f32[128,4,4]{0,2,1:T(4,128)S(1)} %fusion.14, f32[128,4,4]{0,2,1:T(4,128)S(1)} %get-tuple-element.27, pred[512]{0:T(512)(128)(4,1)S(1)} %get-tuple-element.23, bf16[512,4,128,1]{2,1,0,3:T(4,128)(2,1)S(1)} %bitcast.125), kind=kOutput, calls=%fused_computation.29 | convolution fusion | flops 274989056 | bytes 5259776 | tf_op jit(solution)/shard_map/ikgj,jkd->ikgd/dot_general | solution.py:32
  42.6 0.2 copy.42
  42.8 0.1 reshape_squeeze.24
  43.0 0.1 reshape.103
  43.1 0.8 fusion.2
  43.9 1.1 fusion.15
  44.9 1.4 %fusion.18 = bf16[4,128,128,4]{2,1,3,0:T(8,128)(2,1)S(1)} fusion(f32[4,512,128,4]{2,1,3,0:T(8,128)S(1)} %get-tuple-element.26, f32[128,4,4]{0,2,1:T(4,128)S(1)} %fusion.15, f32[128,4,4]{0,2,1:T(4,128)S(1)} %get-tuple-element.25, pred[512]{0:T(512)(128)(4,1)S(1)} %get-tuple-element.24, bf16[512,4,128,1]{2,1,0,3:T(4,128)(2,1)S(1)} %bitcast.124), kind=kOutput, calls=%fused_computation.28 | convolution fusion | flops 274989056 | bytes 5259776 | tf_op jit(solution)/shard_map/ikgj,jkd->ikgd/dot_general | solution.py:32
  46.4 0.2 copy.43
  46.6 0.1 pad_maximum_fusion
  46.7 52.8 %all-gather.2.cloned.1.call-done = bf16[2048,1024]{1,0:T(8,128)(2,1)} async-done(((bf16[256,1024]{1,0:T(8,128)(2,1)}), bf16[2048,1024]{1,0:T(8,128)(2,1)}) %all-gather.2.cloned.1.call-update) | async-done | bytes 4194320 | tf_op jit(solution)/shard_map/all_gather | solution.py:85
  99.5 3.5 %convolution_convert_fusion = bf16[256,1024]{1,0:T(8,128)(2,1)S(1)} fusion(bf16[256,2048]{1,0:T(8,128)(2,1)S(1)} %bitcast.123, bf16[2048,1024]{1,0:T(8,128)(2,1)} %all-gather.2.cloned.1.call-done), kind=kOutput, calls=%fused_computation.30 | convolution fusion | flops 1074003968 | bytes 5767168 | tf_op jit(solution)/shard_map/dot_general | solution.py:83
  103.0 0.4 copy.44
  103.5 4.2 %all_to_all.4 = bf16[2,128,1024]{1,0,2:T(2,128)(2,1)S(1)} all-to-all(bf16[2,128,1024]{1,0,2:T(2,128)(2,1)S(1)} %copy.44), channel_id=1, replica_groups=mesh['clip'=2,'tm'=8,'tile'=2] {'tile'}, dimensions={2} | all-to-all | bytes 1048576 | tf_op jit(solution)/shard_map/all_to_all | solution.py:91
  107.6 0.5 copy.85
  108.2 0.8 reshape.95
  109.0 0.8 reshape.94
  109.8 0.1 multiply_reduce_fusion
  110.0 0.2 fusion.27
  110.2 0.7 collective-permute-start.4
  110.9 0.2 multiply_convert_fusion
  111.1 0.0 collective-permute-done.4
  111.2 1.6 %bitcast_reduce_fusion.1 = (f32[256,8]{0,1:T(8,128)S(1)}, f32[8,768,256]{2,1,0:T(8,128)S(1)}) fusion(pred[768]{0:T(1024)(128)(4,1)S(1)} %pad_add_fusion, bf16[256,8,64]{0,2,1:T(8,128)(2,1)S(1)} %get-tuple-element.13, bf16[256,8,64]{0,2,1:T(8,128)(2,1)S(1)} %bitcast.133), kind=kOutput, calls=%fused_computation.4 | convolution fusion | flops 208402432 | bytes 6824704 | tf_op jit(solution)/shard_map/ihd,jhd->ihj/dot_general | solution.py:113
  112.8 1.5 %fusion.23 = bf16[8,64,256]{2,1,0:T(8,128)(2,1)S(1)} fusion(f32[8,768,256]{2,1,0:T(8,128)S(1)} %get-tuple-element.32, f32[256,8]{0,1:T(8,128)S(1)} %get-tuple-element.31, pred[768]{0:T(1024)(128)(4,1)S(1)} %pad_add_fusion, bf16[256,8,64]{0,2,1:T(8,128)(2,1)S(1)} %bitcast.134, bf16[256,8,64]{0,2,1:T(8,128)(2,1)S(1)} %get-tuple-element.13), kind=kOutput, calls=%fused_computation.32 | convolution fusion | flops 210108416 | bytes 7086848 | tf_op jit(solution)/shard_map/ihj,jhd->ihd/dot_general | solution.py:118
  114.3 0.1 copy.48
  114.4 1.6 %bitcast_reduce_fusion = (f32[256,8]{0,1:T(8,128)S(1)}, f32[8,768,256]{2,1,0:T(8,128)S(1)}) fusion(pred[768]{0:T(1024)(128)(4,1)S(1)} %pad_add_fusion.1, bf16[256,8,64]{0,2,1:T(8,128)(2,1)S(1)} %get-tuple-element.14, bf16[256,8,64]{0,2,1:T(8,128)(2,1)S(1)} %bitcast.131), kind=kOutput, calls=%fused_computation.1 | convolution fusion | flops 208402432 | bytes 6824704 | tf_op jit(solution)/shard_map/ihd,jhd->ihj/dot_general | solution.py:113
  116.0 1.5 %fusion.20 = bf16[8,64,256]{2,1,0:T(8,128)(2,1)S(1)} fusion(f32[8,768,256]{2,1,0:T(8,128)S(1)} %get-tuple-element.30, f32[256,8]{0,1:T(8,128)S(1)} %get-tuple-element.29, pred[768]{0:T(1024)(128)(4,1)S(1)} %pad_add_fusion.1, bf16[256,8,64]{0,2,1:T(8,128)(2,1)S(1)} %bitcast.132, bf16[256,8,64]{0,2,1:T(8,128)(2,1)S(1)} %get-tuple-element.14), kind=kOutput, calls=%fused_computation.31 | convolution fusion | flops 210108416 | bytes 7086848 | tf_op jit(solution)/shard_map/ihj,jhd->ihd/dot_general | solution.py:118
  117.5 0.1 copy.49
  117.7 0.8 pad_maximum_fusion.7
  (10 shorter events, 0.1 us)
Async XLA Ops:
  6.5 28.2 %copy-start.2 = (s32[2]{0:T(128)S(1)}, s32[2]{0:T(128)}, u32[]{:S(2)}) copy-start(s32[2]{0:T(128)} %param.9) | copy-start | bytes 28
  6.5 30.4 %copy-start = (bf16[2,2,128,512]{3,2,1,0:T(8,128)(2,1)S(1)}, bf16[2,2,128,512]{3,2,1,0:T(8,128)(2,1)}, u32[]{:S(2)}) copy-start(bf16[2,2,128,512]{3,2,1,0:T(8,128)(2,1)} %param.6) | copy-start | bytes 1572868
  6.5 24.7 %copy-start.1 = (f32[512]{0:T(512)S(1)}, f32[512]{0:T(512)}, u32[]{:S(2)}) copy-start(f32[512]{0:T(512)} %param.8) | copy-start | bytes 6148
  6.5 93.0 %all-gather.2.cloned.1.call-start = ((), (), s32[]{:S(2)}) async-start(), calls=%async_computation.1 | async-start | bytes 4718592 | tf_op jit(solution)/shard_map/all_gather | solution.py:85
  10.9 23.8 %collective-permute-start.3 = (s32[2]{0:T(128)}, s32[2]{0:T(128)S(1)}, u32[]{:S(2)}, u32[]{:S(2)}) collective-permute-start(s32[2]{0:T(128)} %param.9), channel_id=1, source_target_pairs={{0,2},{2,4},{4,6},{6,8},{8,10},{10,12},{12,14},{1,3},{3,5},{5,7},{... | collective-permute-start | bytes 32 | tf_op jit(solution)/shard_map/ppermute | solution.py:17
  15.4 16.6 %collective-permute-start.5 = (s32[2]{0:T(128)}, s32[2]{0:T(128)S(1)}, u32[]{:S(2)}, u32[]{:S(2)}) collective-permute-start(s32[2]{0:T(128)} %param.9), channel_id=1, source_target_pairs={} | collective-permute-start | bytes 32 | tf_op jit(solution)/shard_map/ppermute | solution.py:17
  16.0 20.8 %collective-permute-start.1 = (bf16[2,2,128,512]{3,2,1,0:T(8,128)(2,1)}, bf16[2,2,128,512]{3,2,1,0:T(8,128)(2,1)S(1)}, u32[]{:S(2)}, u32[]{:S(2)}) collective-permute-start(bf16[2,2,128,512]{3,2,1,0:T(8,128)(2,1)} %param.6), channel_id=1, source_target_pairs={{0,2},{2,4},{4,6},{6,8},{8,10},{10,12},{12,14},{1,3},{3,5},{5,7},{... | collective-permute-start | bytes 1572872 | tf_op jit(solution)/shard_map/ppermute | solution.py:17
  20.5 16.2 %collective-permute-start = (bf16[2,1,128,512]{3,2,1,0:T(8,128)(2,1)S(1)}, bf16[2,1,128,512]{3,2,1,0:T(8,128)(2,1)S(1)}, u32[]{:S(2)}, u32[]{:S(2)}) collective-permute-start(bf16[2,1,128,512]{3,2,1,0:T(8,128)(2,1)S(1)} %slice.65), channel_id=1, source_target_pairs={{0,4},{2,6},{4,8},{6,10},{8,12},{10,14},{1,5},{3,7},{5,9},{7,11},{... | collective-permute-start | bytes 786440 | tf_op jit(solution)/shard_map/ppermute | solution.py:17
  25.4 10.5 %collective-permute-start.2 = (s32[1]{0:T(128)}, s32[1]{0:T(128)}, u32[]{:S(2)}, u32[]{:S(2)}) collective-permute-start(s32[1]{0:T(128)} %get-tuple-element.20), channel_id=1, source_target_pairs={{0,4},{2,6},{4,8},{6,10},{8,12},{10,14},{1,5},{3,7},{5,9},{7,11},{... | collective-permute-start | bytes 20 | tf_op jit(solution)/shard_map/ppermute | solution.py:17
  110.2 0.9 collective-permute-start.4
Sparse Core Ops, SparseCore 0:
  11.0 88.5 all-gather.1
where the time goes:
time: 126 us; the launch traced here: 125 us
  waiting for transfers between devices  54.1 us (43%)
  starting transfers between devices  16.8 us (13%)
  matrix products  15.1 us (12%)
  between operations  13.8 us (11%)
  local copies, waits for them, and re-layouts  10 us (8%)
  blocking collectives  8.45 us (7%)
  other arithmetic  7.11 us (6%)
    all_gather x1, waiting for transfers between devices, local(): lax.all_gather(full_columns, 'tm', axis=0, tiled=True)  52.8 us
    ppermute x6, starting transfers between devices, passed_along(): lax.ppermute(value, axis, [(source, source + steps) for source in range(i...  16.8 us
    all_gather x1, blocking collectives, local(): full_columns = lax.all_gather(proj_weight, 'tile', axis=1, tiled=True)  4.3 us
    all_to_all x1, blocking collectives, local(): lax.all_to_all(own_latent, 'tile', split_axis=2, concat_axis=1, tiled=True)  4.15 us
    dot_general x1, matrix products, local(): jnp.dot(token_rows, lax.all_gather(full_columns, 'tm', axis=0, tiled=True...  3.48 us
    dot_general x2, matrix products, local(): jnp.einsum('ihd,jhd->ihj', query_rows, key_rows, preferred_element_type=j...  3.23 us
    dot_general x2, matrix products, local(): jnp.einsum('ihj,jhd->ihd', normalized, key_rows, preferred_element_type=j...  2.96 us
    dot_general x2, matrix products, window_attention(): jnp.einsum('ikgj,jkd->ikgd', normalized, value_block, preferred_element_t...  2.82 us
  transfers between devices with their start and end apart: 7, of which 3 were waited for; matrix products, arithmetic and copies ran while one was open for 15% of the time, Pallas kernels for 0%

commit v1 on v0

v1 whole, which is shorter than its diff:
```python
import functools
import math

import jax
import jax.numpy as jnp
from jax import lax
from jax.experimental import pallas as pl
from jax.experimental.pallas import tpu as pltpu
from jax.sharding import PartitionSpec as P

QHEADS = 16
KVHEADS = 4
HEAD_DIM = 128
IDM_DIM = 64
WINDOW = 4
PARTNER = 16
LEAD = WINDOW - 1
LANES = 128
TILE_ROWS = 16
DEAD = -1e30
LOG2E = math.log2(math.e)
MESH = pl.DeviceIdType.MESH


def passed_along(value, axis, steps):
    count = lax.axis_size(axis)
    initial, last = (max(0, -steps), min(count, count - steps))
    return lax.ppermute(value, axis, [(source, source + steps) for source in range(initial, last)])


def columns_of(mesh):
    place = mesh.axis_names.index("tm")
    line = mesh.devices.transpose(
        [place] + [i for i in range(mesh.devices.ndim) if i != place]
    ).reshape(mesh.shape["tm"], -1)[:, 0]
    coords = [getattr(device, "coords", None) for device in line]
    if coords[0] is None or len(line) == 1:
        return 1
    moved = [i for i in range(len(coords[0])) if coords[0][i] != coords[1][i]]
    if len(moved) != 1:
        return 1
    columns = len({c[moved[0]] for c in coords})
    return columns if len(line) % columns == 0 else 1


def halo_plan(frames):
    plan, covered, hop = [], 0, 1
    while covered < LEAD:
        needed = min(frames, LEAD - covered)
        covered += needed
        plan.append((hop, needed, LEAD - covered))
        hop += 1
    return plan


def ring_chunks(rows, clip, clips):
    third = (rows // TILE_ROWS // 3) * TILE_ROWS if clips == 2 else 0
    chunks = []
    if third:
        chunks.append((clip * (rows - third), third, True))
    chunks.append((third, rows - 2 * third, False))
    return chunks


def latent_kernel(
    n, clips, tiles, x_count,
    counts_ref, q_ref, kv_ref, w_ref, gain_ref, out_ref,
    q_buf, kv_win, w_full, att, counts, bias,
    local_sem, halo_send, halo_recv, count_send, count_recv,
    ring_send, ring_recv, clip_send, clip_recv, tile_send, tile_recv,
):
    clip, tm, tile = lax.axis_index("clip"), lax.axis_index("tm"), lax.axis_index("tile")
    frames, tokens, width = q_ref.shape
    rows = w_ref.shape[0]
    groups = QHEADS // KVHEADS
    plan = halo_plan(frames)
    z_count = n // x_count

    def place_of(index):
        x, z = lax.rem(index, x_count), index // x_count
        return x * z_count + z + lax.rem(x, 2) * (z_count - 1 - 2 * z)

    def index_of(place):
        place = lax.rem(place + 2 * n, n)
        x, z = place // z_count, lax.rem(place, z_count)
        return (z + lax.rem(x, 2) * (z_count - 1 - 2 * z)) * x_count + x

    place = place_of(tm)
    ends = (index_of(place + 1), index_of(place - 1))

    own_copies = [
        pltpu.make_async_copy(kv_ref, kv_win.at[:, LEAD:LEAD + frames], local_sem.at[0]),
        pltpu.make_async_copy(q_ref, q_buf, local_sem.at[1]),
        pltpu.make_async_copy(w_ref, w_full.at[tm], local_sem.at[2]),
    ]
    for copy in own_copies:
        copy.start()

    barrier = pltpu.get_barrier_semaphore()
    expected = 0
    if n > 1:
        for end in ends:
            pl.semaphore_signal(barrier, inc=1, device_id={"tm": end}, device_id_type=MESH)
            expected += 1
    if clips == 2:
        pl.semaphore_signal(barrier, inc=1, device_id={"clip": 1 - clip}, device_id_type=MESH)
        expected += 1
    if tiles == 2:
        pl.semaphore_signal(barrier, inc=1, device_id={"tile": 1 - tile}, device_id_type=MESH)
        expected += 1
    for hop, _, _ in plan:
        @pl.when(tm + hop < n)
        def _():
            pl.semaphore_signal(barrier, inc=1, device_id={"tm": tm + hop}, device_id_type=MESH)

        @pl.when(tm >= hop)
        def _():
            pl.semaphore_signal(barrier, inc=1, device_id={"tm": tm - hop}, device_id_type=MESH)

        expected = expected + jnp.where(tm + hop < n, 1, 0) + jnp.where(tm >= hop, 1, 0)
    for f in range(frames):
        counts[0, f:f + 1, :] = jnp.full((1, LANES), counts_ref[f], jnp.int32)
    pl.semaphore_wait(barrier, expected)

    halo = []
    for i, (hop, needed, start) in enumerate(plan):
        target = {"tm": lax.rem(tm + hop, n)}
        halo.append((
            hop,
            pltpu.make_async_remote_copy(
                src_ref=kv_ref.at[:, frames - needed:frames],
                dst_ref=kv_win.at[:, start:start + needed],
                send_sem=halo_send.at[i], recv_sem=halo_recv.at[i],
                device_id=target, device_id_type=MESH),
            pltpu.make_async_remote_copy(
                src_ref=counts.at[0], dst_ref=counts.at[hop],
                send_sem=count_send.at[i], recv_sem=count_recv.at[i],
                device_id=target, device_id_type=MESH),
        ))
    for hop, kv_copy, count_copy in halo:
        @pl.when(tm + hop < n)
        def _():
            count_copy.start()
            kv_copy.start()

    chunks = ring_chunks(rows, clip, clips)
    steps = n // 2
    started, later = [], []

    def ring_copy(way, step, c):
        start, size, _ = chunks[c]
        owner = index_of(place - step * (1 - 2 * way))
        span = pl.ds(start if isinstance(start, int) else pl.multiple_of(start, TILE_ROWS), size)
        slot = (way * max(steps, 1) + step) * len(chunks) + c
        return pltpu.make_async_remote_copy(
            src_ref=w_ref.at[span] if step == 0 else w_full.at[owner, span],
            dst_ref=w_full.at[owner, span],
            send_sem=ring_send.at[slot], recv_sem=ring_recv.at[slot],
            device_id={"tm": ends[way]}, device_id_type=MESH)

    def goes(way, step, c):
        return n % 2 == 1 or step < steps - 1 or c % 2 == way

    def send_step(way, step, c):
        if step < steps and goes(way, step, c):
            copy = ring_copy(way, step, c)
            copy.start()
            started.append(copy)

    def take_step(step):
        for c in range(len(chunks)):
            for way in range(2):
                if not goes(way, step, c):
                    continue
                ring_copy(way, step, c).wait_recv()
                send_step(way, step + 1, c)
                start, size, over = chunks[c]
                if over:
                    owner = index_of(place - (step + 1) * (1 - 2 * way))
                    span = pl.ds(pl.multiple_of(start, TILE_ROWS), size)
                    slot = way * max(steps, 1) + step
                    copy = pltpu.make_async_remote_copy(
                        src_ref=w_full.at[owner, span], dst_ref=w_full.at[owner, span],
                        send_sem=clip_send.at[slot], recv_sem=clip_recv.at[slot],
                        device_id={"clip": 1 - clip}, device_id_type=MESH)
                    copy.start()
                    later.append(copy)

    if steps:
        for c in range(len(chunks)):
            for way in range(2):
                send_step(way, 0, c)

    for hop, kv_copy, count_copy in halo:
        _, needed, start = plan[hop - 1]

        @pl.when(tm < hop)
        def _():
            counts[hop] = jnp.zeros(counts.shape[1:], jnp.int32)
            kv_win[:, start:start + needed] = jnp.zeros(
                (2, needed) + kv_win.shape[2:], kv_win.dtype)

    taken = 0
    if steps > 1:
        take_step(0)
        taken = 1

    for hop, kv_copy, count_copy in halo:
        @pl.when(tm >= hop)
        def _():
            count_copy.wait_recv()
            kv_copy.wait_recv()
    own_copies[0].wait()
    own_copies[1].wait()

    slots = tile * tokens + lax.broadcasted_iota(jnp.int32, (tokens, LANES), 0)
    first_lane = lax.broadcasted_iota(jnp.int32, (tokens, LANES), 1) == 0
    for w in range(LEAD + frames):
        if w >= LEAD:
            row = counts[0, w - LEAD:w - LEAD + 1, :]
        else:
            hop, needed, start = [p for p in plan if p[2] <= w < p[2] + p[1]][0]
            at = frames - needed + w - start
            row = counts[hop, at:at + 1, :]
        bias[w] = jnp.where(
            jnp.logical_and(first_lane, slots >= row), DEAD, 0.0).astype(bias.dtype)

    keys = WINDOW * tokens
    unit_lane = (
        lax.broadcasted_iota(jnp.int32, (groups * tokens, LANES), 1) == 0
    ).astype(jnp.bfloat16)
    ones = jnp.ones((keys, LANES), jnp.bfloat16)
    scale = HEAD_DIM ** (-0.5) * LOG2E
    exchanged = []
    units = frames * KVHEADS
    every = max(1, units // max(1, steps))
    for unit in range(units):
        f, g = unit // KVHEADS, unit % KVHEADS
        span = slice(g * HEAD_DIM, (g + 1) * HEAD_DIM)
        k = kv_win[0, f:f + WINDOW, :, span].reshape(keys, HEAD_DIM)
        v = kv_win[1, f:f + WINDOW, :, span].reshape(keys, HEAD_DIM)
        k = jnp.concatenate([k, bias[f:f + WINDOW].reshape(keys, LANES)], axis=1)
        v = jnp.concatenate([v, ones], axis=1)
        q = jnp.concatenate(
            [q_buf[f, :, (g * groups + i) * HEAD_DIM:(g * groups + i + 1) * HEAD_DIM]
             for i in range(groups)], axis=0)
        q = jnp.concatenate([q, unit_lane], axis=1)
        scores = lax.dot_general(q, k, (((1,), (1,)), ((), ())), preferred_element_type=jnp.float32)
        top = jnp.max(scores, axis=-1, keepdims=True)
        weights = jnp.exp2((scores - top) * scale).astype(jnp.bfloat16)
        mixed = jnp.dot(weights, v, preferred_element_type=jnp.float32)
        result = (mixed[:, :HEAD_DIM] / mixed[:, HEAD_DIM:]).astype(jnp.bfloat16)
        for i in range(groups):
            at = (g * groups + i) * HEAD_DIM
            att[f, tile, :, at:at + HEAD_DIM] = result[i * tokens:(i + 1) * tokens]
        if tiles == 2:
            part = att.at[f, tile, :, g * groups * HEAD_DIM:(g + 1) * groups * HEAD_DIM]
            copy = pltpu.make_async_remote_copy(
                src_ref=part, dst_ref=part,
                send_sem=tile_send.at[unit], recv_sem=tile_recv.at[unit],
                device_id={"tile": 1 - tile}, device_id_type=MESH)
            copy.start()
            exchanged.append(copy)
        if unit % every == every - 1 and taken < steps - 1:
            take_step(taken)
            taken += 1
    while taken < steps:
        take_step(taken)
        taken += 1

    own_copies[2].wait()
    for copy in exchanged:
        copy.wait_recv()
    for copy in later:
        copy.wait_recv()

    columns = w_ref.shape[1]
    same = (
        lax.rem(lax.broadcasted_iota(jnp.int32, (2 * LANES, LANES), 0), LANES) // IDM_DIM
        == lax.broadcasted_iota(jnp.int32, (2 * LANES, LANES), 1) // IDM_DIM
    ).astype(jnp.bfloat16)
    weight = w_full[...].reshape(n * rows, columns)
    for f in range(frames):
        token_rows = att[f].reshape(tiles * tokens, width)
        latent = jnp.dot(token_rows, weight, preferred_element_type=jnp.float32)
        latent = latent.astype(jnp.bfloat16).astype(jnp.float32)
        for c in range(0, columns, LANES):
            value = latent[:, c:c + LANES]
            square = value * value
            high = square.astype(jnp.bfloat16)
            low = (square - high.astype(jnp.float32)).astype(jnp.bfloat16)
            total = jnp.dot(
                jnp.concatenate([high, low], axis=1), same, preferred_element_type=jnp.float32)
            scaled = value * lax.rsqrt(total * (1.0 / IDM_DIM) + 1e-6) * gain_ref[:, c:c + LANES]
            out_ref[f, :, c:c + LANES] = scaled.astype(out_ref.dtype)

    for copy in started + later + exchanged:
        copy.wait_send()
    for hop, kv_copy, count_copy in halo:
        @pl.when(tm + hop < n)
        def _():
            count_copy.wait_send()
            kv_copy.wait_send()


def normed_latent(mesh, queries, keyvals, proj_weight, norm_gain, frame_counts):
    n, clips, tiles = (mesh.shape[a] for a in ("tm", "clip", "tile"))
    frames, tokens, width = queries.shape
    rows, columns = proj_weight.shape
    hops = len(halo_plan(frames))
    steps = max(1, n // 2)
    units = frames * KVHEADS
    dma = pltpu.SemaphoreType.DMA
    any_spec = pl.BlockSpec(memory_space=pl.ANY)
    vmem = pl.BlockSpec(memory_space=pltpu.VMEM)
    bf16 = jnp.bfloat16
    flops = frames * tokens * width * 4 * WINDOW * tokens + 2 * frames * tiles * tokens * width * columns
    return pl.pallas_call(
        functools.partial(latent_kernel, n, clips, tiles, columns_of(mesh)),
        out_shape=jax.ShapeDtypeStruct((frames, tiles * tokens, columns), bf16),
        in_specs=[pl.BlockSpec(memory_space=pltpu.SMEM), any_spec, any_spec, any_spec, vmem],
        out_specs=vmem,
        scratch_shapes=[
            pltpu.VMEM(queries.shape, bf16),
            pltpu.VMEM((2, LEAD + frames) + keyvals.shape[2:], bf16),
            pltpu.VMEM((n, rows, columns), bf16),
            pltpu.VMEM((frames, tiles, tokens, width), bf16),
            pltpu.VMEM((hops + 1, max(8, frames), LANES), jnp.int32),
            pltpu.VMEM((LEAD + frames, tokens, LANES), bf16),
            dma((3,)), dma((hops,)), dma((hops,)), dma((hops,)), dma((hops,)),
            dma((4 * steps,)), dma((4 * steps,)), dma((2 * steps,)), dma((2 * steps,)),
            dma((units,)), dma((units,)),
        ],
        compiler_params=pltpu.CompilerParams(
            collective_id=0, has_side_effects=True, vmem_limit_bytes=48 * 2 ** 20),
        cost_estimate=pl.CostEstimate(
            flops=flops, bytes_accessed=8 * 2 ** 20, transcendentals=0),
    )(frame_counts, queries, keyvals, proj_weight, norm_gain.reshape(1, -1))


def partner_kernel(sources, counts_ref, *refs):
    out_ref = refs[-1]
    frame = pl.program_id(0)
    tokens, columns = out_ref.shape[1:]
    keys = sources * tokens
    slots = lax.broadcasted_iota(jnp.int32, (tokens, LANES), 0)
    live = jnp.concatenate(
        [slots < counts_ref[source, frame] for source in range(sources)], axis=0)
    lower = lax.broadcasted_iota(jnp.int32, (tokens, LANES), 1) < IDM_DIM
    scale = IDM_DIM ** (-0.5) * LOG2E
    for c in range(0, columns, LANES):
        k = jnp.concatenate([ref[0, :, c:c + LANES] for ref in refs[:sources]], axis=0)
        q = refs[0][0, :, c:c + LANES]
        zero = jnp.zeros_like(q)
        q = jnp.concatenate([jnp.where(lower, q, zero), jnp.where(lower, zero, q)], axis=0)
        v = jnp.concatenate(
            [jnp.where(live, k, jnp.zeros_like(k)), live.astype(k.dtype)], axis=1)
        scores = lax.dot_general(q, k, (((1,), (1,)), ((), ())), preferred_element_type=jnp.float32)
        weights = jnp.exp2(scores * scale).astype(jnp.bfloat16)
        mixed = jnp.dot(weights, v, preferred_element_type=jnp.float32)
        result = mixed[:, :LANES] / mixed[:, LANES:]
        out_ref[0, :, c:c + LANES] = jnp.where(
            lower, result[:tokens], result[tokens:]).astype(out_ref.dtype)


def partner_attention(counts, blocks):
    frames, tokens, columns = blocks[0].shape
    spec = pl.BlockSpec((1, tokens, columns), lambda f: (f, 0, 0))
    return pl.pallas_call(
        functools.partial(partner_kernel, len(blocks)),
        out_shape=jax.ShapeDtypeStruct(blocks[0].shape, jnp.bfloat16),
        grid=(frames,),
        in_specs=[pl.BlockSpec(memory_space=pltpu.SMEM)] + [spec] * len(blocks),
        out_specs=spec,
        compiler_params=pltpu.CompilerParams(vmem_limit_bytes=32 * 2 ** 20),
    )(counts, *blocks)


def local(mesh, queries, keyvals, proj_weight, norm_gain, frame_counts):
    normed = normed_latent(mesh, queries, keyvals, proj_weight, norm_gain, frame_counts)
    distance = PARTNER // queries.shape[0]
    blocks, counts = [normed], [frame_counts]
    for steps in (distance, -distance):
        if distance < mesh.shape["tm"]:
            block, count = passed_along((normed, frame_counts), "tm", steps)
            blocks.append(block)
            counts.append(count)
    return partner_attention(jnp.stack(counts), blocks)


def solution(mesh):
    in_specs = (
        P(("clip", "tm"), "tile", None),
        P(None, ("clip", "tm"), "tile", None),
        P("tm", "tile"),
        P("tile"),
        P(("clip", "tm")),
    )
    out_specs = P(("clip", "tm"), None, "tile")
    return jax.shard_map(
        functools.partial(local, mesh), mesh=mesh, in_specs=in_specs, out_specs=out_specs,
        check_vma=False)
```

time: 126 us -> 50.9 us (0.40)
  the two profiles are of different devices: /device:TPU:0 before, /device:TPU:24 now
where the time goes in v1:
time: 50.9 us; the launch traced here: 50.6 us
  Pallas kernels  46.7 us (92%)
  local copies, waits for them, and re-layouts  3.9 us (8%)
    pallas_call x1, Pallas kernels, normed_latent(): pl.pallas_call(functools.partial(latent_kernel, n, clips, tiles, columns_...  43.8 us
    unnamed x10, local copies, waits for them, and re-layouts  3.9 us
    pallas_call x1, Pallas kernels, partner_attention(): pl.pallas_call(functools.partial(partner_kernel, len(blocks)), out_shape=...  2.96 us

profile of v1, /device:TPU:24, one launch (start us, length us, event | category | flops | bytes accessed | tf_op | source)
XLA Modules:
  0.0 50.6 jit_solution(14395281645220853698)
XLA Ops:
  0.0 0.0 copy-start.4
  0.0 0.0 copy-start
  0.0 0.7 %copy-done.4 = f32[512]{0:T(512)S(1)} copy-done((f32[512]{0:T(512)S(1)}, f32[512]{0:T(512)}, u32[]{:S(2)}) %copy-start.4) | copy-done | bytes 2072
  0.7 0.0 copy-done
  0.7 0.0 copy-start.1
  0.7 1.2 %copy-done.1 = bf16[2,128,2048]{2,1,0:T(8,128)(2,1)S(1)} copy-done((bf16[2,128,2048]{2,1,0:T(8,128)(2,1)S(1)}, bf16[2,128,2048]{2,1,0:T(8,128)(2,1)}, u32[]{:S(2)}) %copy-start.1) | copy-done | bytes 1048600
  1.9 0.0 copy-start.2
  1.9 1.0 %copy-done.2 = bf16[2,2,128,512]{3,2,1,0:T(8,128)(2,1)S(1)} copy-done((bf16[2,2,128,512]{3,2,1,0:T(8,128)(2,1)S(1)}, bf16[2,2,128,512]{3,2,1,0:T(8,128)(2,1)}, u32[]{:S(2)}) %copy-start.2) | copy-done | bytes 524312
  3.0 0.0 copy-start.3
  3.0 0.9 %copy-done.3 = bf16[256,512]{1,0:T(8,128)(2,1)S(1)} copy-done((bf16[256,512]{1,0:T(8,128)(2,1)S(1)}, bf16[256,512]{1,0:T(8,128)(2,1)}, u32[]{:S(2)}) %copy-start.3) | copy-done | bytes 262168
  3.9 43.8 %shard_map.55.refs_0_ = bf16[2,256,512]{2,1,0:T(8,128)(2,1)S(1)} custom-call(s32[2]{0:T(128)S(1)} %copy-done, bf16[2,128,2048]{2,1,0:T(8,128)(2,1)S(1)} %copy-done.1, bf16[2,2,128,512]{3,2,1,0:T(8,128)(2,1)S(1)} %copy-done.2, bf16[256,512]{1,0:T(8,128)(2,1)S(1)} %copy-done.3, f32[1,512]{1,0:T(1,128)S(1)} %bitcast.3), custom_call_target="tpu_custom_call" | custom-call | flops 2147483648 | bytes 8388608 | tf_op jit(solution)/shard_map/pallas_call | solution.py:318
  47.7 3.0 %shard_map.56 = bf16[2,256,512]{2,1,0:T(8,128)(2,1)} custom-call(s32[1,2]{1,0:T(1,128)S(1)} %bitcast.2, bf16[2,256,512]{2,1,0:T(8,128)(2,1)S(1)} %shard_map.55.refs_0_), custom_call_target="tpu_custom_call" | custom-call | tf_op jit(solution)/shard_map/pallas_call | solution.py:369
Async XLA Ops:
  0.0 0.7 %copy-start.4 = (f32[512]{0:T(512)S(1)}, f32[512]{0:T(512)}, u32[]{:S(2)}) copy-start(f32[512]{0:T(512)} %param.8) | copy-start | bytes 6148
  0.0 0.7 %copy-start = (s32[2]{0:T(128)S(1)}, s32[2]{0:T(128)}, u32[]{:S(2)}) copy-start(s32[2]{0:T(128)} %counts_ref.1) | copy-start | bytes 28
  0.7 1.2 %copy-start.1 = (bf16[2,128,2048]{2,1,0:T(8,128)(2,1)S(1)}, bf16[2,128,2048]{2,1,0:T(8,128)(2,1)}, u32[]{:S(2)}) copy-start(bf16[2,128,2048]{2,1,0:T(8,128)(2,1)} %q_ref.1) | copy-start | bytes 3145732
  1.9 1.0 %copy-start.2 = (bf16[2,2,128,512]{3,2,1,0:T(8,128)(2,1)S(1)}, bf16[2,2,128,512]{3,2,1,0:T(8,128)(2,1)}, u32[]{:S(2)}) copy-start(bf16[2,2,128,512]{3,2,1,0:T(8,128)(2,1)} %kv_ref.1) | copy-start | bytes 1572868
  3.0 0.9 %copy-start.3 = (bf16[256,512]{1,0:T(8,128)(2,1)S(1)}, bf16[256,512]{1,0:T(8,128)(2,1)}, u32[]{:S(2)}) copy-start(bf16[256,512]{1,0:T(8,128)(2,1)} %w_ref.1) | copy-start | bytes 786436

commit v2 on v1

--- a/solution.py
+++ b/solution.py
@@ -53,19 +53,22 @@
     return plan
 
 
+def relayed(plan, x_count, n):
+    return x_count == 2 and n % 2 == 0 and len(plan) == 2 and plan[0][1] > plan[1][1]
+
+
 def ring_chunks(rows, clip, clips):
-    third = (rows // TILE_ROWS // 3) * TILE_ROWS if clips == 2 else 0
-    chunks = []
-    if third:
-        chunks.append((clip * (rows - third), third, True))
-    chunks.append((third, rows - 2 * third, False))
-    return chunks
+    over = clips == 2 and rows % (2 * TILE_ROWS) == 0
+    start, size = (clip * (rows // 2), rows // 2) if over else (0, rows)
+    if size % (2 * TILE_ROWS):
+        return [(start, size, over)]
+    return [(start, size // 2, over), (start + size // 2, size // 2, over)]
 
 
 def latent_kernel(
     n, clips, tiles, x_count,
     counts_ref, q_ref, kv_ref, w_ref, gain_ref, out_ref,
-    q_buf, kv_win, w_full, att, counts, bias,
+    q_buf, kv_win, stash, w_full, att, counts, bias,
     local_sem, halo_send, halo_recv, count_send, count_recv,
     ring_send, ring_recv, clip_send, clip_recv, tile_send, tile_recv,
 ):
@@ -122,26 +125,73 @@
         counts[0, f:f + 1, :] = jnp.full((1, LANES), counts_ref[f], jnp.int32)
     pl.semaphore_wait(barrier, expected)
 
-    halo = []
-    for i, (hop, needed, start) in enumerate(plan):
-        target = {"tm": lax.rem(tm + hop, n)}
-        halo.append((
-            hop,
-            pltpu.make_async_remote_copy(
-                src_ref=kv_ref.at[:, frames - needed:frames],
-                dst_ref=kv_win.at[:, start:start + needed],
-                send_sem=halo_send.at[i], recv_sem=halo_recv.at[i],
-                device_id=target, device_id_type=MESH),
-            pltpu.make_async_remote_copy(
-                src_ref=counts.at[0], dst_ref=counts.at[hop],
-                send_sem=count_send.at[i], recv_sem=count_recv.at[i],
-                device_id=target, device_id_type=MESH),
-        ))
-    for hop, kv_copy, count_copy in halo:
-        @pl.when(tm + hop < n)
-        def _():
-            count_copy.start()
-            kv_copy.start()
+    count_copies = []
+    for i, (hop, _, _) in enumerate(plan):
+        count_copies.append((hop, pltpu.make_async_remote_copy(
+            src_ref=counts.at[0], dst_ref=counts.at[hop],
+            send_sem=count_send.at[i], recv_sem=count_recv.at[i],
+            device_id={"tm": lax.rem(tm + hop, n)}, device_id_type=MESH)))
+    for hop, copy in count_copies:
+        pl.when(tm + hop < n)(copy.start)
+
+    def halo_copy(role, arrival, g, source, first, count, place_at, hop):
+        span = pl.ds(g * HEAD_DIM, HEAD_DIM)
+        target = stash if place_at is None else kv_win.at[:, place_at:place_at + count]
+        return pltpu.make_async_remote_copy(
+            src_ref=source.at[:, first:first + count, :, span],
+            dst_ref=target.at[:, :, :, span],
+            send_sem=halo_send.at[role * KVHEADS + g],
+            recv_sem=halo_recv.at[arrival * KVHEADS + g],
+            device_id={"tm": lax.rem(tm + hop + n, n)}, device_id_type=MESH)
+
+    firsts, relays, arrivals = [], [], []
+    if relayed(plan, x_count, n):
+        (_, needed, start), (_, last, start2) = plan
+        rest = needed - last
+        even, odd = lax.rem(tm, 2) == 0, lax.rem(tm, 2) == 1
+        up, down = tm + 2 < n, tm >= 2
+        for g in range(KVHEADS):
+            firsts += [
+                (halo_copy(2, 2, g, kv_ref, frames - last, last, start2, 2), up),
+                (halo_copy(3, 3, g, kv_ref, frames - needed, rest, None, -1),
+                 jnp.logical_and(odd, up)),
+                (halo_copy(0, 0, g, kv_ref, frames - needed, rest, start, 1), even),
+                (halo_copy(1, 1, g, kv_ref, frames - last, last, start + rest, 1), even),
+            ]
+            relays.append([
+                (halo_copy(4, 0, g, stash, 0, rest, start, 2), jnp.logical_and(even, up), 3),
+                (halo_copy(5, 1, g, kv_win, start2, last, start + rest, -1),
+                 jnp.logical_and(odd, down), 2),
+            ])
+            arrivals.append([
+                (0, tm >= 1, rest, start), (1, tm >= 1, last, start + rest),
+                (2, jnp.logical_and(even, down), last, start2),
+            ])
+    else:
+        for g in range(KVHEADS):
+            for i, (hop, needed, start) in enumerate(plan):
+                firsts.append((
+                    halo_copy(i, i, g, kv_ref, frames - needed, needed, start, hop), tm + hop < n))
+            relays.append([])
+            arrivals.append([
+                (i, tm >= hop, needed, start) for i, (hop, needed, start) in enumerate(plan)])
+    for copy, mine in firsts:
+        pl.when(mine)(copy.start)
+
+    def arrival_of(arrival, g, count, place_at):
+        return halo_copy(0, arrival, g, kv_ref, 0, count, place_at, 1)
+
+    def relay(g):
+        for copy, mine, arrival in relays[g]:
+            @pl.when(mine)
+            def _():
+                count, place_at = (rest, None) if arrival == 3 else (last, start2)
+                arrival_of(arrival, g, count, place_at).wait_recv()
+                copy.start()
+
+    def arrive(g):
+        for arrival, mine, count, place_at in arrivals[g]:
+            pl.when(mine)(arrival_of(arrival, g, count, place_at).wait_recv)
 
     chunks = ring_chunks(rows, clip, clips)
     steps = n // 2
@@ -178,7 +228,7 @@
                 if over:
                     owner = index_of(place - (step + 1) * (1 - 2 * way))
                     span = pl.ds(pl.multiple_of(start, TILE_ROWS), size)
-                    slot = way * max(steps, 1) + step
+                    slot = (way * steps + step) * len(chunks) + c
                     copy = pltpu.make_async_remote_copy(
                         src_ref=w_full.at[owner, span], dst_ref=w_full.at[owner, span],
                         send_sem=clip_send.at[slot], recv_sem=clip_recv.at[slot],
@@ -191,25 +241,15 @@
             for way in range(2):
                 send_step(way, 0, c)
 
-    for hop, kv_copy, count_copy in halo:
-        _, needed, start = plan[hop - 1]
-
+    for hop, needed, start in plan:
         @pl.when(tm < hop)
         def _():
             counts[hop] = jnp.zeros(counts.shape[1:], jnp.int32)
             kv_win[:, start:start + needed] = jnp.zeros(
                 (2, needed) + kv_win.shape[2:], kv_win.dtype)
 
-    taken = 0
-    if steps > 1:
-        take_step(0)
-        taken = 1
-
-    for hop, kv_copy, count_copy in halo:
-        @pl.when(tm >= hop)
-        def _():
-            count_copy.wait_recv()
-            kv_copy.wait_recv()
+    for hop, copy in count_copies:
+        pl.when(tm >= hop)(copy.wait_recv)
     own_copies[0].wait()
     own_copies[1].wait()
 
@@ -232,10 +272,17 @@
     ones = jnp.ones((keys, LANES), jnp.bfloat16)
     scale = HEAD_DIM ** (-0.5) * LOG2E
     exchanged = []
-    units = frames * KVHEADS
-    every = max(1, units // max(1, steps))
-    for unit in range(units):
-        f, g = unit // KVHEADS, unit % KVHEADS
+    taken = 0
+    relay(0)
+    for unit in range(KVHEADS * frames):
+        g, f = unit // frames, unit % frames
+        if f == 0:
+            if taken < steps - 1:
+                take_step(taken)
+                taken += 1
+            if g + 1 < KVHEADS:
+                relay(g + 1)
+            arrive(g)
         span = slice(g * HEAD_DIM, (g + 1) * HEAD_DIM)
         k = kv_win[0, f:f + WINDOW, :, span].reshape(keys, HEAD_DIM)
         v = kv_win[1, f:f + WINDOW, :, span].reshape(keys, HEAD_DIM)
@@ -261,9 +308,6 @@
                 device_id={"tile": 1 - tile}, device_id_type=MESH)
             copy.start()
             exchanged.append(copy)
-        if unit % every == every - 1 and taken < steps - 1:
-            take_step(taken)
-            taken += 1
     while taken < steps:
         take_step(taken)
         taken += 1
@@ -296,18 +340,20 @@
 
     for copy in started + later + exchanged:
         copy.wait_send()
-    for hop, kv_copy, count_copy in halo:
-        @pl.when(tm + hop < n)
-        def _():
-            count_copy.wait_send()
-            kv_copy.wait_send()
+    for hop, copy in count_copies:
+        pl.when(tm + hop < n)(copy.wait_send)
+    for copy, mine in firsts + [entry[:2] for group in relays for entry in group]:
+        pl.when(mine)(copy.wait_send)
 
 
 def normed_latent(mesh, queries, keyvals, proj_weight, norm_gain, frame_counts):
     n, clips, tiles = (mesh.shape[a] for a in ("tm", "clip", "tile"))
     frames, tokens, width = queries.shape
     rows, columns = proj_weight.shape
-    hops = len(halo_plan(frames))
+    plan = halo_plan(frames)
+    hops = len(plan)
+    rest = max(1, plan[0][1] - plan[1][1]) if hops > 1 else 1
+    roles = max(6, hops) * KVHEADS
     steps = max(1, n // 2)
     units = frames * KVHEADS
     dma = pltpu.SemaphoreType.DMA
@@ -323,16 +369,17 @@
         scratch_shapes=[
             pltpu.VMEM(queries.shape, bf16),
             pltpu.VMEM((2, LEAD + frames) + keyvals.shape[2:], bf16),
+            pltpu.VMEM((2, rest) + keyvals.shape[2:], bf16),
             pltpu.VMEM((n, rows, columns), bf16),
             pltpu.VMEM((frames, tiles, tokens, width), bf16),
             pltpu.VMEM((hops + 1, max(8, frames), LANES), jnp.int32),
             pltpu.VMEM((LEAD + frames, tokens, LANES), bf16),
-            dma((3,)), dma((hops,)), dma((hops,)), dma((hops,)), dma((hops,)),
-            dma((4 * steps,)), dma((4 * steps,)), dma((2 * steps,)), dma((2 * steps,)),
+            dma((3,)), dma((roles,)), dma((roles,)), dma((hops,)), dma((hops,)),
+            dma((4 * steps,)), dma((4 * steps,)), dma((4 * steps,)), dma((4 * steps,)),
             dma((units,)), dma((units,)),
         ],
         compiler_params=pltpu.CompilerParams(
-            collective_id=0, has_side_effects=True, vmem_limit_bytes=48 * 2 ** 20),
+            collective_id=0, has_side_effects=True, vmem_limit_bytes=60 * 2 ** 20),
         cost_estimate=pl.CostEstimate(
             flops=flops, bytes_accessed=8 * 2 ** 20, transcendentals=0),
     )(frame_counts, queries, keyvals, proj_weight, norm_gain.reshape(1, -1))

time: 50.9 us -> 45.3 us (0.89); the launches traced: 50.6 us -> 44.4 us
  Pallas kernels: 46.7 us -> 43.3 us
  local copies, waits for them, and re-layouts: 3.9 us -> 1.04 us
    pallas_call x1, Pallas kernels: 43.8 us -> 40.4 us  [normed_latent(): pl.pallas_call(functools.partial(latent_kernel, n, clips, tiles, columns_...]
    unnamed x10 -> x4, local copies, waits for them, and re-layouts: 3.9 us -> 1.04 us
where the time goes in v2:
time: 45.3 us; the launch traced here: 44.4 us
  Pallas kernels  43.3 us (96%)
  local copies, waits for them, and re-layouts  1.04 us (2%)
    pallas_call x1, Pallas kernels, normed_latent(): pl.pallas_call(functools.partial(latent_kernel, n, clips, tiles, columns_...  40.4 us
    pallas_call x1, Pallas kernels, partner_attention(): pl.pallas_call(functools.partial(partner_kernel, len(blocks)), out_shape=...  2.93 us
    unnamed x4, local copies, waits for them, and re-layouts  1.04 us

profile of v2, /device:TPU:24, one launch (start us, length us, event | category | flops | bytes accessed | tf_op | source)
XLA Modules:
  0.0 44.4 jit_solution(1559049998680311181)
XLA Ops:
  0.0 0.0 copy-start.1
  0.0 40.4 %shard_map.55.refs_0_ = bf16[2,256,512]{2,1,0:T(8,128)(2,1)} custom-call(s32[2]{0:T(128)} %counts_ref.1, bf16[2,128,2048]{2,1,0:T(8,128)(2,1)} %q_ref.1, bf16[2,2,128,512]{3,2,1,0:T(8,128)(2,1)} %kv_ref.1, bf16[256,512]{1,0:T(8,128)(2,1)} %w_ref.1, f32[1,512]{1,0:T(1,128)} %bitcast.3), custom_call_target="tpu_custom_call" | custom-call | flops 2147483648 | bytes 8388608 | tf_op jit(solution)/shard_map/pallas_call | solution.py:364
  40.4 0.0 copy-done.1
  40.4 0.0 copy-start
  40.4 1.0 %copy-done = bf16[2,256,512]{2,1,0:T(8,128)(2,1)S(1)} copy-done((bf16[2,256,512]{2,1,0:T(8,128)(2,1)S(1)}, bf16[2,256,512]{2,1,0:T(8,128)(2,1)}, u32[]{:S(2)}) %copy-start) | copy-done | bytes 524312
  41.5 2.9 %shard_map.56 = bf16[2,256,512]{2,1,0:T(8,128)(2,1)} custom-call(s32[1,2]{1,0:T(1,128)S(1)} %bitcast.2, bf16[2,256,512]{2,1,0:T(8,128)(2,1)S(1)} %copy-done), custom_call_target="tpu_custom_call" | custom-call | tf_op jit(solution)/shard_map/pallas_call | solution.py:416
Async XLA Ops:
  0.0 40.4 %copy-start.1 = (s32[2]{0:T(128)S(1)}, s32[2]{0:T(128)}, u32[]{:S(2)}) copy-start(s32[2]{0:T(128)} %counts_ref.1) | copy-start | bytes 28
  40.4 1.0 %copy-start = (bf16[2,256,512]{2,1,0:T(8,128)(2,1)S(1)}, bf16[2,256,512]{2,1,0:T(8,128)(2,1)}, u32[]{:S(2)}) copy-start(bf16[2,256,512]{2,1,0:T(8,128)(2,1)} %shard_map.55.refs_0_) | copy-start | bytes 1572868

commit v3 on v2

--- a/solution.py
+++ b/solution.py
@@ -68,7 +68,7 @@
 def latent_kernel(
     n, clips, tiles, x_count,
     counts_ref, q_ref, kv_ref, w_ref, gain_ref, out_ref,
-    q_buf, kv_win, stash, w_full, att, counts, bias,
+    q_buf, kv_win, stash, w_full, att, total_ref, counts, bias,
     local_sem, halo_send, halo_recv, count_send, count_recv,
     ring_send, ring_recv, clip_send, clip_recv, tile_send, tile_recv,
 ):
@@ -144,14 +144,14 @@
             recv_sem=halo_recv.at[arrival * KVHEADS + g],
             device_id={"tm": lax.rem(tm + hop + n, n)}, device_id_type=MESH)
 
-    firsts, relays, arrivals = [], [], []
+    firsts, relays, arrivals = [[] for _ in range(KVHEADS)], [], []
     if relayed(plan, x_count, n):
         (_, needed, start), (_, last, start2) = plan
         rest = needed - last
         even, odd = lax.rem(tm, 2) == 0, lax.rem(tm, 2) == 1
         up, down = tm + 2 < n, tm >= 2
         for g in range(KVHEADS):
-            firsts += [
+            firsts[g] += [
                 (halo_copy(2, 2, g, kv_ref, frames - last, last, start2, 2), up),
                 (halo_copy(3, 3, g, kv_ref, frames - needed, rest, None, -1),
                  jnp.logical_and(odd, up)),
@@ -170,13 +170,16 @@
     else:
         for g in range(KVHEADS):
             for i, (hop, needed, start) in enumerate(plan):
-                firsts.append((
+                firsts[g].append((
                     halo_copy(i, i, g, kv_ref, frames - needed, needed, start, hop), tm + hop < n))
             relays.append([])
             arrivals.append([
                 (i, tm >= hop, needed, start) for i, (hop, needed, start) in enumerate(plan)])
-    for copy, mine in firsts:
-        pl.when(mine)(copy.start)
+
+    def issue(g):
+        if g < KVHEADS:
+            for copy, mine in firsts[g]:
+                pl.when(mine)(copy.start)
 
     def arrival_of(arrival, g, count, place_at):
         return halo_copy(0, arrival, g, kv_ref, 0, count, place_at, 1)
@@ -236,10 +239,11 @@
                     copy.start()
                     later.append(copy)
 
-    if steps:
-        for c in range(len(chunks)):
-            for way in range(2):
-                send_step(way, 0, c)
+    issue(0)
+    for c in range(len(chunks)):
+        for way in range(2):
+            send_step(way, 0, c)
+    issue(1)
 
     for hop, needed, start in plan:
         @pl.when(tm < hop)
@@ -273,15 +277,14 @@
     scale = HEAD_DIM ** (-0.5) * LOG2E
     exchanged = []
     taken = 0
-    relay(0)
     for unit in range(KVHEADS * frames):
         g, f = unit // frames, unit % frames
         if f == 0:
+            relay(g)
             if taken < steps - 1:
                 take_step(taken)
                 taken += 1
-            if g + 1 < KVHEADS:
-                relay(g + 1)
+            issue(g + 2)
             arrive(g)
         span = slice(g * HEAD_DIM, (g + 1) * HEAD_DIM)
         k = kv_win[0, f:f + WINDOW, :, span].reshape(keys, HEAD_DIM)
@@ -308,25 +311,54 @@
                 device_id={"tile": 1 - tile}, device_id_type=MESH)
             copy.start()
             exchanged.append(copy)
-    while taken < steps:
+    while taken < steps - 1:
         take_step(taken)
         taken += 1
-
-    own_copies[2].wait()
-    for copy in exchanged:
-        copy.wait_recv()
-    for copy in later:
-        copy.wait_recv()
 
     columns = w_ref.shape[1]
     same = (
         lax.rem(lax.broadcasted_iota(jnp.int32, (2 * LANES, LANES), 0), LANES) // IDM_DIM
         == lax.broadcasted_iota(jnp.int32, (2 * LANES, LANES), 1) // IDM_DIM
     ).astype(jnp.bfloat16)
-    weight = w_full[...].reshape(n * rows, columns)
+    own_copies[2].wait()
+    for copy in exchanged:
+        copy.wait_recv()
+
+    def projected(f, owners):
+        if owners is None:
+            return jnp.dot(
+                att[f].reshape(tiles * tokens, width), w_full[...].reshape(n * rows, columns),
+                preferred_element_type=jnp.float32)
+        parts = []
+        for owner in owners:
+            span = pl.ds(pl.multiple_of(owner * rows, LANES), rows)
+            parts.append(jnp.dot(
+                att[f, :, :, span].reshape(tiles * tokens, rows), w_full[owner],
+                preferred_element_type=jnp.float32))
+        return sum(parts)
+
+    first_wave, last_wave = [tm], None
+    by_clip = list(later)
+    if rows % LANES == 0 and steps > 1:
+        for step in range(steps - 1):
+            first_wave += [index_of(place - step - 1), index_of(place + step + 1)]
+        last_wave = [index_of(place - steps)]
+        if n % 2:
+            last_wave.append(index_of(place + steps))
+        for copy in by_clip:
+            copy.wait_recv()
+        for f in range(frames):
+            total_ref[f] = projected(f, first_wave)
+    else:
+        by_clip = []
+    if steps:
+        take_step(steps - 1)
+    for copy in later[len(by_clip):]:
+        copy.wait_recv()
     for f in range(frames):
-        token_rows = att[f].reshape(tiles * tokens, width)
-        latent = jnp.dot(token_rows, weight, preferred_element_type=jnp.float32)
+        latent = projected(f, last_wave)
+        if last_wave is not None:
+            latent = latent + total_ref[f]
         latent = latent.astype(jnp.bfloat16).astype(jnp.float32)
         for c in range(0, columns, LANES):
             value = latent[:, c:c + LANES]
@@ -342,8 +374,9 @@
         copy.wait_send()
     for hop, copy in count_copies:
         pl.when(tm + hop < n)(copy.wait_send)
-    for copy, mine in firsts + [entry[:2] for group in relays for entry in group]:
-        pl.when(mine)(copy.wait_send)
+    for group in firsts + relays:
+        for entry in group:
+            pl.when(entry[1])(entry[0].wait_send)
 
 
 def normed_latent(mesh, queries, keyvals, proj_weight, norm_gain, frame_counts):
@@ -357,14 +390,14 @@
     steps = max(1, n // 2)
     units = frames * KVHEADS
     dma = pltpu.SemaphoreType.DMA
-    any_spec = pl.BlockSpec(memory_space=pl.ANY)
+    hbm = pl.BlockSpec(memory_space=pltpu.HBM)
     vmem = pl.BlockSpec(memory_space=pltpu.VMEM)
     bf16 = jnp.bfloat16
     flops = frames * tokens * width * 4 * WINDOW * tokens + 2 * frames * tiles * tokens * width * columns
     return pl.pallas_call(
         functools.partial(latent_kernel, n, clips, tiles, columns_of(mesh)),
         out_shape=jax.ShapeDtypeStruct((frames, tiles * tokens, columns), bf16),
-        in_specs=[pl.BlockSpec(memory_space=pltpu.SMEM), any_spec, any_spec, any_spec, vmem],
+        in_specs=[pl.BlockSpec(memory_space=pltpu.SMEM), hbm, hbm, hbm, vmem],
         out_specs=vmem,
         scratch_shapes=[
             pltpu.VMEM(queries.shape, bf16),
@@ -372,6 +405,7 @@
             pltpu.VMEM((2, rest) + keyvals.shape[2:], bf16),
             pltpu.VMEM((n, rows, columns), bf16),
             pltpu.VMEM((frames, tiles, tokens, width), bf16),
+            pltpu.VMEM((frames, tiles * tokens, columns), jnp.float32),
             pltpu.VMEM((hops + 1, max(8, frames), LANES), jnp.int32),
             pltpu.VMEM((LEAD + frames, tokens, LANES), bf16),
             dma((3,)), dma((roles,)), dma((roles,)), dma((hops,)), dma((hops,)),
@@ -419,7 +453,7 @@
         grid=(frames,),
         in_specs=[pl.BlockSpec(memory_space=pltpu.SMEM)] + [spec] * len(blocks),
         out_specs=spec,
-        compiler_params=pltpu.CompilerParams(vmem_limit_bytes=32 * 2 ** 20),
+        compiler_params=pltpu.CompilerParams(vmem_limit_bytes=60 * 2 ** 20),
     )(counts, *blocks)
 
 

time: 45.3 us -> 42 us (0.927)
  the two profiles are of different devices: /device:TPU:24 before, /device:TPU:17 now
where the time goes in v3:
time: 42 us; the launch traced here: 41.9 us
  Pallas kernels  41.9 us (100%)
    pallas_call x1, Pallas kernels, normed_latent(): pl.pallas_call(functools.partial(latent_kernel, n, clips, tiles, columns_...  38.5 us
    pallas_call x1, Pallas kernels, partner_attention(): pl.pallas_call(functools.partial(partner_kernel, len(blocks)), out_shape=...  3.36 us

profile of v3, /device:TPU:17, one launch (start us, length us, event | category | flops | bytes accessed | tf_op | source)
XLA Modules:
  0.0 41.9 jit_solution(15013793356562775105)
XLA Ops:
  0.0 38.5 %shard_map.55.refs_0_ = bf16[2,256,512]{2,1,0:T(8,128)(2,1)} custom-call(s32[2]{0:T(128)} %counts_ref.1, bf16[2,128,2048]{2,1,0:T(8,128)(2,1)} %q_ref.1, bf16[2,2,128,512]{3,2,1,0:T(8,128)(2,1)} %kv_ref.1, bf16[256,512]{1,0:T(8,128)(2,1)} %w_ref.1, f32[1,512]{1,0:T(1,128)} %bitcast.3), custom_call_target="tpu_custom_call" | custom-call | flops 2147483648 | bytes 8388608 | tf_op jit(solution)/shard_map/pallas_call | solution.py:397
  38.5 3.4 %shard_map.56 = bf16[2,256,512]{2,1,0:T(8,128)(2,1)} custom-call(s32[1,2]{1,0:T(1,128)} %bitcast.2, bf16[2,256,512]{2,1,0:T(8,128)(2,1)} %shard_map.55.refs_0_), custom_call_target="tpu_custom_call" | custom-call | tf_op jit(solution)/shard_map/pallas_call | solution.py:450

commit v4 on v3

--- a/solution.py
+++ b/solution.py
@@ -220,8 +220,8 @@
             copy.start()
             started.append(copy)
 
-    def take_step(step):
-        for c in range(len(chunks)):
+    def take(step, c):
+        if c < len(chunks):
             for way in range(2):
                 if not goes(way, step, c):
                     continue
@@ -239,10 +239,11 @@
                     copy.start()
                     later.append(copy)
 
-    issue(0)
     for c in range(len(chunks)):
         for way in range(2):
             send_step(way, 0, c)
+        if c == 0:
+            issue(0)
     issue(1)
 
     for hop, needed, start in plan:
@@ -277,15 +278,20 @@
     scale = HEAD_DIM ** (-0.5) * LOG2E
     exchanged = []
     taken = 0
+    relay(0)
     for unit in range(KVHEADS * frames):
         g, f = unit // frames, unit % frames
         if f == 0:
-            relay(g)
             if taken < steps - 1:
-                take_step(taken)
-                taken += 1
+                take(taken, 0)
             issue(g + 2)
             arrive(g)
+        if f == frames - 1:
+            if taken < steps - 1:
+                take(taken, 1)
+                taken += 1
+            if g + 1 < KVHEADS:
+                relay(g + 1)
         span = slice(g * HEAD_DIM, (g + 1) * HEAD_DIM)
         k = kv_win[0, f:f + WINDOW, :, span].reshape(keys, HEAD_DIM)
         v = kv_win[1, f:f + WINDOW, :, span].reshape(keys, HEAD_DIM)
@@ -311,8 +317,10 @@
                 device_id={"tile": 1 - tile}, device_id_type=MESH)
             copy.start()
             exchanged.append(copy)
-    while taken < steps - 1:
-        take_step(taken)
+    while taken < steps:
+        before_last = list(later)
+        take(taken, 0)
+        take(taken, 1)
         taken += 1
 
     columns = w_ref.shape[1]
@@ -338,7 +346,7 @@
         return sum(parts)
 
     first_wave, last_wave = [tm], None
-    by_clip = list(later)
+    by_clip = before_last if steps else []
     if rows % LANES == 0 and steps > 1:
         for step in range(steps - 1):
             first_wave += [index_of(place - step - 1), index_of(place + step + 1)]
@@ -351,8 +359,6 @@
             total_ref[f] = projected(f, first_wave)
     else:
         by_clip = []
-    if steps:
-        take_step(steps - 1)
     for copy in later[len(by_clip):]:
         copy.wait_recv()
     for f in range(frames):

time: 42 us -> 40.7 us (0.969)
  the two profiles are of different devices: /device:TPU:17 before, /device:TPU:24 now
where the time goes in v4:
time: 40.7 us; the launch traced here: 40.6 us
  Pallas kernels  40.6 us (100%)
    pallas_call x1, Pallas kernels, normed_latent(): pl.pallas_call(functools.partial(latent_kernel, n, clips, tiles, columns_...  37.2 us
    pallas_call x1, Pallas kernels, partner_attention(): pl.pallas_call(functools.partial(partner_kernel, len(blocks)), out_shape=...  3.36 us

profile of v4, /device:TPU:24, one launch (start us, length us, event | category | flops | bytes accessed | tf_op | source)
XLA Modules:
  0.0 40.6 jit_solution(16696858087149904686)
XLA Ops:
  0.0 37.2 %shard_map.55.refs_0_ = bf16[2,256,512]{2,1,0:T(8,128)(2,1)} custom-call(s32[2]{0:T(128)} %counts_ref.1, bf16[2,128,2048]{2,1,0:T(8,128)(2,1)} %q_ref.1, bf16[2,2,128,512]{3,2,1,0:T(8,128)(2,1)} %kv_ref.1, bf16[256,512]{1,0:T(8,128)(2,1)} %w_ref.1, f32[1,512]{1,0:T(1,128)} %bitcast.3), custom_call_target="tpu_custom_call" | custom-call | flops 2147483648 | bytes 8388608 | tf_op jit(solution)/shard_map/pallas_call | solution.py:403
  37.2 3.4 %shard_map.56 = bf16[2,256,512]{2,1,0:T(8,128)(2,1)} custom-call(s32[1,2]{1,0:T(1,128)} %bitcast.2, bf16[2,256,512]{2,1,0:T(8,128)(2,1)} %shard_map.55.refs_0_), custom_call_target="tpu_custom_call" | custom-call | tf_op jit(solution)/shard_map/pallas_call | solution.py:456

commit v5 on v4

--- a/solution.py
+++ b/solution.py
@@ -58,11 +58,17 @@
 
 
 def ring_chunks(rows, clip, clips):
-    over = clips == 2 and rows % (2 * TILE_ROWS) == 0
-    start, size = (clip * (rows // 2), rows // 2) if over else (0, rows)
-    if size % (2 * TILE_ROWS):
-        return [(start, size, over)]
-    return [(start, size // 2, over), (start + size // 2, size // 2, over)]
+    over = rows * 7 // 16 // TILE_ROWS * TILE_ROWS if clips == 2 else 0
+    ahead = -(-over // 2 // TILE_ROWS) * TILE_ROWS
+    if not over or ahead == over:
+        half = rows // 2 // TILE_ROWS * TILE_ROWS
+        return [(at, size, 0, 0) for at, size in ((0, half), (half, rows - half)) if size]
+    first = clip * (rows - ahead)
+    return [
+        (first, ahead, first, ahead),
+        (ahead + clip * (over - ahead), rows - over - ahead,
+         ahead + clip * (rows - over - ahead), over - ahead),
+    ]
 
 
 def latent_kernel(
@@ -201,7 +207,7 @@
     started, later = [], []
 
     def ring_copy(way, step, c):
-        start, size, _ = chunks[c]
+        start, size, _, _ = chunks[c]
         owner = index_of(place - step * (1 - 2 * way))
         span = pl.ds(start if isinstance(start, int) else pl.multiple_of(start, TILE_ROWS), size)
         slot = (way * max(steps, 1) + step) * len(chunks) + c
@@ -227,8 +233,8 @@
                     continue
                 ring_copy(way, step, c).wait_recv()
                 send_step(way, step + 1, c)
-                start, size, over = chunks[c]
-                if over:
+                _, _, start, size = chunks[c]
+                if size:
                     owner = index_of(place - (step + 1) * (1 - 2 * way))
                     span = pl.ds(pl.multiple_of(start, TILE_ROWS), size)
                     slot = (way * steps + step) * len(chunks) + c
@@ -445,9 +451,9 @@
         scores = lax.dot_general(q, k, (((1,), (1,)), ((), ())), preferred_element_type=jnp.float32)
         weights = jnp.exp2(scores * scale).astype(jnp.bfloat16)
         mixed = jnp.dot(weights, v, preferred_element_type=jnp.float32)
-        result = mixed[:, :LANES] / mixed[:, LANES:]
-        out_ref[0, :, c:c + LANES] = jnp.where(
-            lower, result[:tokens], result[tokens:]).astype(out_ref.dtype)
+        total = jnp.where(lower, mixed[:tokens, LANES:], mixed[tokens:, LANES:])
+        result = jnp.where(lower, mixed[:tokens, :LANES], mixed[tokens:, :LANES]) / total
+        out_ref[0, :, c:c + LANES] = result.astype(out_ref.dtype)
 
 
 def partner_attention(counts, blocks):

time: 40.7 us -> 41.8 us (1.027)
  Pallas kernels: 40.6 us -> 41.6 us
    pallas_call x1, Pallas kernels: 37.2 us -> 38.3 us  [normed_latent(): pl.pallas_call(functools.partial(latent_kernel, n, clips, tiles, columns_...]
where the time goes in v5:
time: 41.8 us; the launch traced here: 41.6 us
  Pallas kernels  41.6 us (100%)
    pallas_call x1, Pallas kernels, normed_latent(): pl.pallas_call(functools.partial(latent_kernel, n, clips, tiles, columns_...  38.3 us
    pallas_call x1, Pallas kernels, partner_attention(): pl.pallas_call(functools.partial(partner_kernel, len(blocks)), out_shape=...  3.36 us

profile of v5, /device:TPU:24, one launch (start us, length us, event | category | flops | bytes accessed | tf_op | source)
XLA Modules:
  0.0 41.6 jit_solution(7775156342985647819)
XLA Ops:
  0.0 38.3 %shard_map.55.refs_0_ = bf16[2,256,512]{2,1,0:T(8,128)(2,1)} custom-call(s32[2]{0:T(128)} %counts_ref.1, bf16[2,128,2048]{2,1,0:T(8,128)(2,1)} %q_ref.1, bf16[2,2,128,512]{3,2,1,0:T(8,128)(2,1)} %kv_ref.1, bf16[256,512]{1,0:T(8,128)(2,1)} %w_ref.1, f32[1,512]{1,0:T(1,128)} %bitcast.3), custom_call_target="tpu_custom_call" | custom-call | flops 2147483648 | bytes 8388608 | tf_op jit(solution)/shard_map/pallas_call | solution.py:409
  38.3 3.4 %shard_map.56 = bf16[2,256,512]{2,1,0:T(8,128)(2,1)} custom-call(s32[1,2]{1,0:T(1,128)} %bitcast.2, bf16[2,256,512]{2,1,0:T(8,128)(2,1)} %shard_map.55.refs_0_), custom_call_target="tpu_custom_call" | custom-call | tf_op jit(solution)/shard_map/pallas_call | solution.py:462

commit v6 on v4

--- a/solution.py
+++ b/solution.py
@@ -60,9 +60,13 @@
 def ring_chunks(rows, clip, clips):
     over = clips == 2 and rows % (2 * TILE_ROWS) == 0
     start, size = (clip * (rows // 2), rows // 2) if over else (0, rows)
-    if size % (2 * TILE_ROWS):
-        return [(start, size, over)]
-    return [(start, size // 2, over), (start + size // 2, size // 2, over)]
+    pieces = 4
+    while size % (pieces * TILE_ROWS):
+        pieces //= 2
+        if pieces <= 1:
+            return [(start, size, over)]
+    size //= pieces
+    return [(start + i * size, size, over) for i in range(pieces)]
 
 
 def latent_kernel(
@@ -134,11 +138,13 @@
     for hop, copy in count_copies:
         pl.when(tm + hop < n)(copy.start)
 
-    def halo_copy(role, arrival, g, source, first, count, place_at, hop):
+    def halo_copy(role, arrival, g, source, first, count, place_at, hop, pair=(0, 2)):
         span = pl.ds(g * HEAD_DIM, HEAD_DIM)
-        target = stash if place_at is None else kv_win.at[:, place_at:place_at + count]
+        taken_from = pair if source is not stash else (0, 1)
+        target = stash if place_at is None else kv_win.at[
+            pair[0]:pair[1], place_at:place_at + count]
         return pltpu.make_async_remote_copy(
-            src_ref=source.at[:, first:first + count, :, span],
+            src_ref=source.at[taken_from[0]:taken_from[1], first:first + count, :, span],
             dst_ref=target.at[:, :, :, span],
             send_sem=halo_send.at[role * KVHEADS + g],
             recv_sem=halo_recv.at[arrival * KVHEADS + g],
@@ -153,19 +159,28 @@
         for g in range(KVHEADS):
             firsts[g] += [
                 (halo_copy(2, 2, g, kv_ref, frames - last, last, start2, 2), up),
-                (halo_copy(3, 3, g, kv_ref, frames - needed, rest, None, -1),
+                (halo_copy(3, 3, g, kv_ref, frames - needed, rest, None, -1, (0, 1)),
+                 jnp.logical_and(odd, up)),
+                (halo_copy(6, 3, g, kv_ref, frames - needed, rest, None, 2, (1, 2)),
                  jnp.logical_and(odd, up)),
                 (halo_copy(0, 0, g, kv_ref, frames - needed, rest, start, 1), even),
                 (halo_copy(1, 1, g, kv_ref, frames - last, last, start + rest, 1), even),
             ]
+            keys_part, values_part = (0, 1), (1, 2)
             relays.append([
-                (halo_copy(4, 0, g, stash, 0, rest, start, 2), jnp.logical_and(even, up), 3),
+                (halo_copy(4, 0, g, stash, 0, rest, start, 2, keys_part),
+                 jnp.logical_and(even, up), (3, g, rest, None, keys_part)),
+                (halo_copy(7, 6, g, stash, 0, rest, start, -1, values_part),
+                 jnp.logical_and(odd, down), (3, g, rest, None, values_part)),
                 (halo_copy(5, 1, g, kv_win, start2, last, start + rest, -1),
-                 jnp.logical_and(odd, down), 2),
+                 jnp.logical_and(odd, down), (2, g, last, start2)),
             ])
             arrivals.append([
-                (0, tm >= 1, rest, start), (1, tm >= 1, last, start + rest),
-                (2, jnp.logical_and(even, down), last, start2),
+                ((0, g, rest, start), odd),
+                ((0, g, rest, start, keys_part), jnp.logical_and(even, down)),
+                ((6, g, rest, start, values_part), jnp.logical_and(even, down)),
+                ((1, g, last, start + rest), tm >= 1),
+                ((2, g, last, start2), jnp.logical_and(even, down)),
             ])
     else:
         for g in range(KVHEADS):
@@ -174,27 +189,26 @@
                     halo_copy(i, i, g, kv_ref, frames - needed, needed, start, hop), tm + hop < n))
             relays.append([])
             arrivals.append([
-                (i, tm >= hop, needed, start) for i, (hop, needed, start) in enumerate(plan)])
+                ((i, g, needed, start), tm >= hop) for i, (hop, needed, start) in enumerate(plan)])
 
     def issue(g):
         if g < KVHEADS:
             for copy, mine in firsts[g]:
                 pl.when(mine)(copy.start)
 
-    def arrival_of(arrival, g, count, place_at):
-        return halo_copy(0, arrival, g, kv_ref, 0, count, place_at, 1)
+    def arrival_of(arrival, g, count, place_at, pair=(0, 2)):
+        return halo_copy(0, arrival, g, kv_ref, 0, count, place_at, 1, pair)
 
     def relay(g):
         for copy, mine, arrival in relays[g]:
             @pl.when(mine)
             def _():
-                count, place_at = (rest, None) if arrival == 3 else (last, start2)
-                arrival_of(arrival, g, count, place_at).wait_recv()
+                arrival_of(*arrival).wait_recv()
                 copy.start()
 
     def arrive(g):
-        for arrival, mine, count, place_at in arrivals[g]:
-            pl.when(mine)(arrival_of(arrival, g, count, place_at).wait_recv)
+        for arrival, mine in arrivals[g]:
+            pl.when(mine)(arrival_of(*arrival).wait_recv)
 
     chunks = ring_chunks(rows, clip, clips)
     steps = n // 2
@@ -220,8 +234,9 @@
             copy.start()
             started.append(copy)
 
-    def take(step, c):
-        if c < len(chunks):
+    def take(step, part):
+        half = (len(chunks) + 1) // 2
+        for c in range(part * half, min(len(chunks), part * half + half)):
             for way in range(2):
                 if not goes(way, step, c):
                     continue
@@ -242,7 +257,7 @@
     for c in range(len(chunks)):
         for way in range(2):
             send_step(way, 0, c)
-        if c == 0:
+        if c == (len(chunks) - 1) // 2:
             issue(0)
     issue(1)
 
@@ -392,7 +407,7 @@
     plan = halo_plan(frames)
     hops = len(plan)
     rest = max(1, plan[0][1] - plan[1][1]) if hops > 1 else 1
-    roles = max(6, hops) * KVHEADS
+    roles = max(8, hops) * KVHEADS
     steps = max(1, n // 2)
     units = frames * KVHEADS
     dma = pltpu.SemaphoreType.DMA
@@ -408,14 +423,14 @@
         scratch_shapes=[
             pltpu.VMEM(queries.shape, bf16),
             pltpu.VMEM((2, LEAD + frames) + keyvals.shape[2:], bf16),
-            pltpu.VMEM((2, rest) + keyvals.shape[2:], bf16),
+            pltpu.VMEM((1, rest) + keyvals.shape[2:], bf16),
             pltpu.VMEM((n, rows, columns), bf16),
             pltpu.VMEM((frames, tiles, tokens, width), bf16),
             pltpu.VMEM((frames, tiles * tokens, columns), jnp.float32),
             pltpu.VMEM((hops + 1, max(8, frames), LANES), jnp.int32),
             pltpu.VMEM((LEAD + frames, tokens, LANES), bf16),
             dma((3,)), dma((roles,)), dma((roles,)), dma((hops,)), dma((hops,)),
-            dma((4 * steps,)), dma((4 * steps,)), dma((4 * steps,)), dma((4 * steps,)),
+            dma((8 * steps,)), dma((8 * steps,)), dma((8 * steps,)), dma((8 * steps,)),
             dma((units,)), dma((units,)),
         ],
         compiler_params=pltpu.CompilerParams(
@@ -445,9 +460,9 @@
         scores = lax.dot_general(q, k, (((1,), (1,)), ((), ())), preferred_element_type=jnp.float32)
         weights = jnp.exp2(scores * scale).astype(jnp.bfloat16)
         mixed = jnp.dot(weights, v, preferred_element_type=jnp.float32)
-        result = mixed[:, :LANES] / mixed[:, LANES:]
-        out_ref[0, :, c:c + LANES] = jnp.where(
-            lower, result[:tokens], result[tokens:]).astype(out_ref.dtype)
+        total = jnp.where(lower, mixed[:tokens, LANES:], mixed[tokens:, LANES:])
+        result = jnp.where(lower, mixed[:tokens, :LANES], mixed[tokens:, :LANES]) / total
+        out_ref[0, :, c:c + LANES] = result.astype(out_ref.dtype)
 
 
 def partner_attention(counts, blocks):

time: 40.7 us -> 41.5 us (1.020)
  Pallas kernels: 40.6 us -> 41.3 us
    pallas_call x1, Pallas kernels: 37.2 us -> 38 us  [normed_latent(): pl.pallas_call(functools.partial(latent_kernel, n, clips, tiles, columns_...]
where the time goes in v6:
time: 41.5 us; the launch traced here: 41.3 us
  Pallas kernels  41.3 us (100%)
    pallas_call x1, Pallas kernels, normed_latent(): pl.pallas_call(functools.partial(latent_kernel, n, clips, tiles, columns_...  38 us
    pallas_call x1, Pallas kernels, partner_attention(): pl.pallas_call(functools.partial(partner_kernel, len(blocks)), out_shape=...  3.36 us

profile of v6, /device:TPU:24, one launch (start us, length us, event | category | flops | bytes accessed | tf_op | source)
XLA Modules:
  0.0 41.3 jit_solution(16197251042323821176)
XLA Ops:
  0.0 38.0 %shard_map.55.refs_0_ = bf16[2,256,512]{2,1,0:T(8,128)(2,1)} custom-call(s32[2]{0:T(128)} %counts_ref.1, bf16[2,128,2048]{2,1,0:T(8,128)(2,1)} %q_ref.1, bf16[2,2,128,512]{3,2,1,0:T(8,128)(2,1)} %kv_ref.1, bf16[256,512]{1,0:T(8,128)(2,1)} %w_ref.1, f32[1,512]{1,0:T(1,128)} %bitcast.3), custom_call_target="tpu_custom_call" | custom-call | flops 2147483648 | bytes 8388608 | tf_op jit(solution)/shard_map/pallas_call | solution.py:418
  38.0 3.4 %shard_map.56 = bf16[2,256,512]{2,1,0:T(8,128)(2,1)} custom-call(s32[1,2]{1,0:T(1,128)} %bitcast.2, bf16[2,256,512]{2,1,0:T(8,128)(2,1)} %shard_map.55.refs_0_), custom_call_target="tpu_custom_call" | custom-call | tf_op jit(solution)/shard_map/pallas_call | solution.py:471

commit v7 on v4

--- a/solution.py
+++ b/solution.py
@@ -240,11 +240,11 @@
                     later.append(copy)
 
     for c in range(len(chunks)):
+        issue(c)
         for way in range(2):
             send_step(way, 0, c)
-        if c == 0:
-            issue(0)
-    issue(1)
+    for g in range(len(chunks), 3):
+        issue(g)
 
     for hop, needed, start in plan:
         @pl.when(tm < hop)
@@ -284,14 +284,14 @@
         if f == 0:
             if taken < steps - 1:
                 take(taken, 0)
-            issue(g + 2)
+            issue(g + 3)
             arrive(g)
         if f == frames - 1:
+            if g + 1 < KVHEADS:
+                relay(g + 1)
             if taken < steps - 1:
                 take(taken, 1)
                 taken += 1
-            if g + 1 < KVHEADS:
-                relay(g + 1)
         span = slice(g * HEAD_DIM, (g + 1) * HEAD_DIM)
         k = kv_win[0, f:f + WINDOW, :, span].reshape(keys, HEAD_DIM)
         v = kv_win[1, f:f + WINDOW, :, span].reshape(keys, HEAD_DIM)
@@ -452,11 +452,12 @@
 
 def partner_attention(counts, blocks):
     frames, tokens, columns = blocks[0].shape
-    spec = pl.BlockSpec((1, tokens, columns), lambda f: (f, 0, 0))
+    part = 2 * LANES if columns % (2 * LANES) == 0 else columns
+    spec = pl.BlockSpec((1, tokens, part), lambda f, c: (f, 0, c))
     return pl.pallas_call(
         functools.partial(partner_kernel, len(blocks)),
         out_shape=jax.ShapeDtypeStruct(blocks[0].shape, jnp.bfloat16),
-        grid=(frames,),
+        grid=(frames, columns // part),
         in_specs=[pl.BlockSpec(memory_space=pltpu.SMEM)] + [spec] * len(blocks),
         out_specs=spec,
         compiler_params=pltpu.CompilerParams(vmem_limit_bytes=60 * 2 ** 20),

time: 40.7 us -> 40.8 us (level)
    pallas_call x1, Pallas kernels: 3.36 us -> 4.28 us  [partner_attention(): pl.pallas_call(functools.partial(partner_kernel, len(blocks)), out_shape=...]
    pallas_call x1, Pallas kernels: 37.2 us -> 36.3 us  [normed_latent(): pl.pallas_call(functools.partial(latent_kernel, n, clips, tiles, columns_...]
where the time goes in v7:
time: 40.8 us; the launch traced here: 40.6 us
  Pallas kernels  40.6 us (100%)
    pallas_call x1, Pallas kernels, normed_latent(): pl.pallas_call(functools.partial(latent_kernel, n, clips, tiles, columns_...  36.3 us
    pallas_call x1, Pallas kernels, partner_attention(): pl.pallas_call(functools.partial(partner_kernel, len(blocks)), out_shape=...  4.28 us

profile of v7, /device:TPU:24, one launch (start us, length us, event | category | flops | bytes accessed | tf_op | source)
XLA Modules:
  0.0 40.6 jit_solution(8716539150773344265)
XLA Ops:
  0.0 36.3 %shard_map.55.refs_0_ = bf16[2,256,512]{2,1,0:T(8,128)(2,1)} custom-call(s32[2]{0:T(128)} %counts_ref.1, bf16[2,128,2048]{2,1,0:T(8,128)(2,1)} %q_ref.1, bf16[2,2,128,512]{3,2,1,0:T(8,128)(2,1)} %kv_ref.1, bf16[256,512]{1,0:T(8,128)(2,1)} %w_ref.1, f32[1,512]{1,0:T(1,128)} %bitcast.3), custom_call_target="tpu_custom_call" | custom-call | flops 2147483648 | bytes 8388608 | tf_op jit(solution)/shard_map/pallas_call | solution.py:403
  36.3 4.3 %shard_map.56 = bf16[2,256,512]{2,1,0:T(8,128)(2,1)} custom-call(s32[1,2]{1,0:T(1,128)} %bitcast.2, bf16[2,256,512]{2,1,0:T(8,128)(2,1)} %shard_map.55.refs_0_), custom_call_target="tpu_custom_call" | custom-call | tf_op jit(solution)/shard_map/pallas_call | solution.py:457

commit v8 on v7

--- a/solution.py
+++ b/solution.py
@@ -452,12 +452,11 @@
 
 def partner_attention(counts, blocks):
     frames, tokens, columns = blocks[0].shape
-    part = 2 * LANES if columns % (2 * LANES) == 0 else columns
-    spec = pl.BlockSpec((1, tokens, part), lambda f, c: (f, 0, c))
+    spec = pl.BlockSpec((1, tokens, columns), lambda f: (f, 0, 0))
     return pl.pallas_call(
         functools.partial(partner_kernel, len(blocks)),
         out_shape=jax.ShapeDtypeStruct(blocks[0].shape, jnp.bfloat16),
-        grid=(frames, columns // part),
+        grid=(frames,),
         in_specs=[pl.BlockSpec(memory_space=pltpu.SMEM)] + [spec] * len(blocks),
         out_specs=spec,
         compiler_params=pltpu.CompilerParams(vmem_limit_bytes=60 * 2 ** 20),

time: 40.8 us -> 39.9 us (0.978)
  Pallas kernels: 40.6 us -> 39.7 us
    pallas_call x1, Pallas kernels: 4.28 us -> 3.36 us  [partner_attention(): pl.pallas_call(functools.partial(partner_kernel, len(blocks)), out_shape=...]
where the time goes in v8:
time: 39.9 us; the launch traced here: 39.7 us
  Pallas kernels  39.7 us (99%)
    pallas_call x1, Pallas kernels, normed_latent(): pl.pallas_call(functools.partial(latent_kernel, n, clips, tiles, columns_...  36.3 us
    pallas_call x1, Pallas kernels, partner_attention(): pl.pallas_call(functools.partial(partner_kernel, len(blocks)), out_shape=...  3.36 us

profile of v8, /device:TPU:24, one launch (start us, length us, event | category | flops | bytes accessed | tf_op | source)
XLA Modules:
  0.0 39.7 jit_solution(6709192263084778939)
XLA Ops:
  0.0 36.3 %shard_map.55.refs_0_ = bf16[2,256,512]{2,1,0:T(8,128)(2,1)} custom-call(s32[2]{0:T(128)} %counts_ref.1, bf16[2,128,2048]{2,1,0:T(8,128)(2,1)} %q_ref.1, bf16[2,2,128,512]{3,2,1,0:T(8,128)(2,1)} %kv_ref.1, bf16[256,512]{1,0:T(8,128)(2,1)} %w_ref.1, f32[1,512]{1,0:T(1,128)} %bitcast.3), custom_call_target="tpu_custom_call" | custom-call | flops 2147483648 | bytes 8388608 | tf_op jit(solution)/shard_map/pallas_call | solution.py:403
  36.3 3.4 %shard_map.56 = bf16[2,256,512]{2,1,0:T(8,128)(2,1)} custom-call(s32[1,2]{1,0:T(1,128)} %bitcast.2, bf16[2,256,512]{2,1,0:T(8,128)(2,1)} %shard_map.55.refs_0_), custom_call_target="tpu_custom_call" | custom-call | tf_op jit(solution)/shard_map/pallas_call | solution.py:456
